TPU v7x, 128 devices: a whole 4x4x4 slice. The times are simulated.
128 devices in a mesh: row: 16 (over y_hi, x, core), col: 8 (over z, y_lo).
Axes of the slice: x: 4, y: 4 (y_hi: 2, y_lo: 2; y = y_hi * 2 + y_lo), z: 4, core: 2. Of those that a mesh axis runs over, the one named last changes fastest.
Arguments:
- cycle_inter: float32 [1536, 1536, 128], P(None, ('row', 'col')), may hold values from -6 to 6
- integrals: float32 [1536, 1536, 128], P(None, ('row', 'col')), may hold values from -0.005859375 to 0.005859375
Outputs:
- ladder: float32 [128, 128], P('row')
All inputs are finite; a program needn't handle non-finite values.
Results may differ from a plain program's by a relative error of at most 0.0003.
Values sent between devices are 32-bit elements; how exact they have to be, the bound alone decides.
No kernel may reach another device: no remote copies, remote signals or barrier semaphores. Data moves between devices by JAX's collectives and lax.ppermute only.
A program may use at most 128 MiB of HBM per device.

v0:
```python
import jax
import jax.numpy as jnp
from jax import lax
from jax.sharding import PartitionSpec as P


def body(cycle_inter, integrals):
    row_count = lax.axis_size("row")
    col_count = lax.axis_size("col")
    local_width = cycle_inter.shape[1]
    occupied = cycle_inter.shape[2]
    slab_pairs = integrals.shape[2]
    received = lax.all_to_all(cycle_inter, ("row", "col"), split_axis=0, concat_axis=1, tiled=True)
    amplitudes = cycle_inter - jnp.swapaxes(received, 0, 1)
    device_rank = lax.axis_index("row") * col_count + lax.axis_index("col")
    first_column = device_rank * local_width
    column_ids = first_column + jnp.arange(local_width, dtype=jnp.int32)
    block_rows = 128
    needed_blocks = (first_column + local_width + block_rows - 1) // block_rows

    def accumulate(block_index, summed):
        offset = block_index * block_rows
        amp_block = lax.dynamic_slice_in_dim(amplitudes, offset, block_rows, 0)
        integral_block = lax.dynamic_slice_in_dim(integrals, offset, block_rows, 0)
        row_ids = offset + jnp.arange(block_rows, dtype=jnp.int32)
        upper_mask = (row_ids[:, None] < column_ids[None, :]).astype(jnp.float32)
        amp_block = amp_block * upper_mask[:, :, None]
        return summed + jnp.einsum(
            "cdi,cda->ia", amp_block, integral_block, precision=lax.Precision.HIGHEST
        )

    partial_sum = lax.fori_loop(
        0, needed_blocks, accumulate, jnp.zeros((occupied, slab_pairs), jnp.float32)
    )
    owned_rows = occupied // row_count
    summed = lax.psum(partial_sum, ("row", "col"))
    return lax.dynamic_slice_in_dim(summed, lax.axis_index("row") * owned_rows, owned_rows, 0)


def solution(mesh):
    return jax.shard_map(
        body,
        mesh=mesh,
        in_specs=(P(None, ("row", "col"), None), P(None, ("row", "col"), None)),
        out_specs=P("row", None),
        check_vma=False,
    )
```

profile of v0, /device:TPU:1, one launch (start us, length us, event | category | flops | bytes accessed | tf_op | source)
XLA Modules:
  0.0 412.1 jit_solution(1875631772332710024)
XLA Ops:
  6.5 12.7 %copy.7 = f32[1536,12,128]{2,1,0:T(8,128)} copy(f32[1536,12,128]{2,0,1:T(8,128)} %param.4) | data formatting | bytes 18874368 | tf_op args[0]
  19.2 11.9 %all-to-all-start = ((f32[1536,12,128]{2,1,0:T(8,128)}), f32[1536,12,128]{2,1,0:T(8,128)}, u32[]{:S(2)}, u32[]{:S(2)}) async-start(f32[1536,12,128]{2,1,0:T(8,128)} %copy.7), calls=%async_computation | async-start | bytes 25165824 | tf_op jit(solution)/shard_map/all_to_all | solution.py:13
  31.1 0.0 all-reduce.2.cloned.1.call-start
  31.2 165.2 %all-to-all-done = f32[1536,12,128]{2,1,0:T(8,128)} async-done(((f32[1536,12,128]{2,1,0:T(8,128)}), f32[1536,12,128]{2,1,0:T(8,128)}, u32[]{:S(2)}, u32[]{:S(2)}) %all-to-all-start) | async-done | bytes 9437216 | tf_op jit(solution)/shard_map/all_to_all | solution.py:13
  196.3 10.3 %copy.9 = f32[12,128,12,128]{3,2,1,0:T(8,128)} copy(f32[12,128,12,128]{3,2,0,1:T(8,128)} %bitcast.2) | data formatting | bytes 18874368 | tf_op jit(solution)/shard_map/all_to_all | solution.py:13
  206.7 12.0 %all_to_all.16 = f32[12,1536,128]{2,1,0:T(8,128)} reshape(f32[12,128,12,128]{3,2,1,0:T(8,128)} %copy.9) | data formatting | bytes 18874368 | tf_op jit(solution)/shard_map/all_to_all | solution.py:13
  218.7 10.9 %bitcast_subtract_fusion = f32[1536,12,128]{2,0,1:T(8,128)} fusion(f32[1536,12,128]{2,0,1:T(8,128)} %param.4, f32[12,1536,128]{2,1,0:T(8,128)} %all_to_all.16), kind=kLoop, calls=%fused_computation.11 | loop fusion | flops 2359296 | bytes 28311552 | tf_op jit(solution)/shard_map/sub | solution.py:14
  229.6 3.6 while.11
  229.6 1.2 constant_dynamic-slice_fusion.3
  230.8 0.3 copy.15
  231.1 0.1 compare_convert_fusion.2
  231.2 2.1 fusion.12
  233.2 0.0 copy-start
  233.2 0.6 copy-done
  233.9 0.0 all-reduce.2.cloned.1.call-update
  233.9 170.1 %all-reduce.2.cloned.1.call-done = f32[128,128]{1,0:T(8,128)} async-done(((f32[128,128]{1,0:T(8,128)}), f32[128,128]{1,0:T(8,128)}) %all-reduce.2.cloned.1.call-update) | async-done | bytes 65552 | tf_op jit(solution)/shard_map/psum | solution.py:36
  404.0 1.3 constant_dynamic-slice_fusion.1
  (3 shorter events, 0.0 us)
Async XLA Ops:
  19.2 177.2 %all-to-all-start = ((f32[1536,12,128]{2,1,0:T(8,128)}), f32[1536,12,128]{2,1,0:T(8,128)}, u32[]{:S(2)}, u32[]{:S(2)}) async-start(f32[1536,12,128]{2,1,0:T(8,128)} %copy.7), calls=%async_computation | async-start | bytes 25165824 | tf_op jit(solution)/shard_map/all_to_all | solution.py:13
  31.1 372.9 %all-reduce.2.cloned.1.call-start = ((), (), s32[]{:S(2)}) async-start(), calls=%async_computation.1 | async-start | bytes 131072 | tf_op jit(solution)/shard_map/psum | solution.py:36
  233.2 0.6 copy-start
Sparse Core Ops, SparseCore 0:
  234.0 169.9 all-reduce.1
where the time goes:
time: 414 us; the launch traced here: 412 us
  waiting for transfers between devices  335 us (81%)
  local copies, waits for them, and re-layouts  38.3 us (9%)
  between operations  13.4 us (3%)
  starting transfers between devices  11.9 us (3%)
  other arithmetic  11 us (3%)
    psum x1, waiting for transfers between devices, body(): summed = lax.psum(partial_sum, ('row', 'col'))  170 us
    all_to_all x1, waiting for transfers between devices, body(): lax.all_to_all(cycle_inter, ('row', 'col'), split_axis=0, concat_axis=1,...  165 us
    all_to_all x2, local copies, waits for them, and re-layouts, body(): lax.all_to_all(cycle_inter, ('row', 'col'), split_axis=0, concat_axis=1,...  22.3 us
    unnamed x3, local copies, waits for them, and re-layouts  13.3 us
    all_to_all x1, starting transfers between devices, body(): lax.all_to_all(cycle_inter, ('row', 'col'), split_axis=0, concat_axis=1,...  11.9 us
    sub x1, other arithmetic, body(): amplitudes = cycle_inter - jnp.swapaxes(received, 0, 1)  10.9 us
  transfers between devices with their start and end apart: 2, of which 2 were waited for; matrix products, arithmetic and copies ran while one was open for 0% of the time, Pallas kernels for 0%

commit v1 on v0

--- a/solution.py
+++ b/solution.py
@@ -2,6 +2,8 @@
 import jax.numpy as jnp
 from jax import lax
 from jax.sharding import PartitionSpec as P
+
+obtain_groups = lambda mesh_dim, comm_axis, arr: lax.psum(lax.psum(arr, comm_axis), mesh_dim)
 
 
 def body(cycle_inter, integrals):
@@ -33,7 +35,7 @@
         0, needed_blocks, accumulate, jnp.zeros((occupied, slab_pairs), jnp.float32)
     )
     owned_rows = occupied // row_count
-    summed = lax.psum(partial_sum, ("row", "col"))
+    summed = obtain_groups("row", "col", partial_sum)
     return lax.dynamic_slice_in_dim(summed, lax.axis_index("row") * owned_rows, owned_rows, 0)
 
 

time: 414 us -> 478 us (1.15)
  waiting for transfers between devices: 335 us -> 398 us
    psum x1 -> x2, waiting for transfers between devices: 170 us -> 233 us  [the longest x1 133 us: lax.psum(lax.psum(arr, comm_axis), mesh_dim)]
  transfers between devices with their start and end apart: 2 -> 3, of which waited for: 2 -> 3; matrix products, arithmetic and copies ran while one was open for 0% -> 0% of each run, Pallas kernels for 0% -> 0%
where the time goes in v1:
time: 478 us; the launch traced here: 475 us
  waiting for transfers between devices  398 us (83%)
  local copies, waits for them, and re-layouts  38.3 us (8%)
  between operations  13.4 us (3%)
  starting transfers between devices  12 us (3%)
  other arithmetic  11 us (2%)
    all_to_all x1, waiting for transfers between devices, body(): lax.all_to_all(cycle_inter, ('row', 'col'), split_axis=0, concat_axis=1,...  165 us
    psum x1, waiting for transfers between devices, lax.psum(lax.psum(arr, comm_axis), mesh_dim)  133 us
    psum x1, waiting for transfers between devices, lax.psum(arr, comm_axis)  99.9 us
    all_to_all x2, local copies, waits for them, and re-layouts, body(): lax.all_to_all(cycle_inter, ('row', 'col'), split_axis=0, concat_axis=1,...  22.3 us
    unnamed x3, local copies, waits for them, and re-layouts  13.3 us
    all_to_all x1, starting transfers between devices, body(): lax.all_to_all(cycle_inter, ('row', 'col'), split_axis=0, concat_axis=1,...  11.9 us
    sub x1, other arithmetic, body(): amplitudes = cycle_inter - jnp.swapaxes(received, 0, 1)  10.9 us
  transfers between devices with their start and end apart: 3, of which 3 were waited for; matrix products, arithmetic and copies ran while one was open for 0% of the time, Pallas kernels for 0%

profile of v1, /device:TPU:1, one launch (start us, length us, event | category | flops | bytes accessed | tf_op | source)
XLA Modules:
  0.0 474.7 jit_solution(9486146143385767379)
XLA Ops:
  6.5 12.7 %copy.7 = f32[1536,12,128]{2,1,0:T(8,128)} copy(f32[1536,12,128]{2,0,1:T(8,128)} %param.4) | data formatting | bytes 18874368 | tf_op args[0]
  19.2 11.9 %all-to-all-start = ((f32[1536,12,128]{2,1,0:T(8,128)}), f32[1536,12,128]{2,1,0:T(8,128)}, u32[]{:S(2)}, u32[]{:S(2)}) async-start(f32[1536,12,128]{2,1,0:T(8,128)} %copy.7), calls=%async_computation | async-start | bytes 25165824 | tf_op jit(solution)/shard_map/all_to_all | solution.py:15
  31.1 0.0 all-reduce.3.cloned.1.call-start
  31.2 165.2 %all-to-all-done = f32[1536,12,128]{2,1,0:T(8,128)} async-done(((f32[1536,12,128]{2,1,0:T(8,128)}), f32[1536,12,128]{2,1,0:T(8,128)}, u32[]{:S(2)}, u32[]{:S(2)}) %all-to-all-start) | async-done | bytes 9437216 | tf_op jit(solution)/shard_map/all_to_all | solution.py:15
  196.3 10.3 %copy.9 = f32[12,128,12,128]{3,2,1,0:T(8,128)} copy(f32[12,128,12,128]{3,2,0,1:T(8,128)} %bitcast.2) | data formatting | bytes 18874368 | tf_op jit(solution)/shard_map/all_to_all | solution.py:15
  206.7 12.0 %all_to_all.16 = f32[12,1536,128]{2,1,0:T(8,128)} reshape(f32[12,128,12,128]{3,2,1,0:T(8,128)} %copy.9) | data formatting | bytes 18874368 | tf_op jit(solution)/shard_map/all_to_all | solution.py:15
  218.7 10.9 %bitcast_subtract_fusion = f32[1536,12,128]{2,0,1:T(8,128)} fusion(f32[1536,12,128]{2,0,1:T(8,128)} %param.4, f32[12,1536,128]{2,1,0:T(8,128)} %all_to_all.16), kind=kLoop, calls=%fused_computation.11 | loop fusion | flops 2359296 | bytes 28311552 | tf_op jit(solution)/shard_map/sub | solution.py:16
  229.6 3.6 while.11
  229.6 1.2 constant_dynamic-slice_fusion.3
  230.8 0.3 copy.15
  231.1 0.1 compare_convert_fusion.2
  231.2 2.1 fusion.12
  233.2 0.0 copy-start
  233.2 0.6 copy-done
  233.9 0.0 all-reduce.3.cloned.1.call-update
  233.9 0.0 all-reduce.5.cloned.1.call-start
  233.9 99.9 %all-reduce.3.cloned.1.call-done = f32[128,128]{1,0:T(8,128)} async-done(((f32[128,128]{1,0:T(8,128)}), f32[128,128]{1,0:T(8,128)}) %all-reduce.3.cloned.1.call-update) | async-done | bytes 65552 | tf_op jit(solution)/shard_map/psum | solution.py:6
  333.9 0.0 all-reduce.5.cloned.1.call-update
  333.9 132.7 %all-reduce.5.cloned.1.call-done = f32[128,128]{1,0:T(8,128)} async-done(((f32[128,128]{1,0:T(8,128)}), f32[128,128]{1,0:T(8,128)}) %all-reduce.5.cloned.1.call-update) | async-done | bytes 65552 | tf_op jit(solution)/shard_map/psum | solution.py:6
  466.6 1.3 constant_dynamic-slice_fusion.1
  (3 shorter events, 0.0 us)
Async XLA Ops:
  19.2 177.2 %all-to-all-start = ((f32[1536,12,128]{2,1,0:T(8,128)}), f32[1536,12,128]{2,1,0:T(8,128)}, u32[]{:S(2)}, u32[]{:S(2)}) async-start(f32[1536,12,128]{2,1,0:T(8,128)} %copy.7), calls=%async_computation | async-start | bytes 25165824 | tf_op jit(solution)/shard_map/all_to_all | solution.py:15
  31.1 302.8 %all-reduce.3.cloned.1.call-start = ((), (), s32[]{:S(2)}) async-start(), calls=%async_computation.1 | async-start | bytes 131072 | tf_op jit(solution)/shard_map/psum | solution.py:6
  233.2 0.6 copy-start
  233.9 232.7 %all-reduce.5.cloned.1.call-start = ((), (), s32[]{:S(2)}) async-start(), calls=%async_computation.2 | async-start | bytes 131072 | tf_op jit(solution)/shard_map/psum | solution.py:6
Sparse Core Ops, SparseCore 0:
  234.0 99.7 all-reduce.2
  336.5 130.0 all-reduce.4

commit v2 on v0

--- a/solution.py
+++ b/solution.py
@@ -33,7 +33,8 @@
         0, needed_blocks, accumulate, jnp.zeros((occupied, slab_pairs), jnp.float32)
     )
     owned_rows = occupied // row_count
-    summed = lax.psum(partial_sum, ("row", "col"))
+    blocks = lax.all_gather(partial_sum, ("row", "col"))
+    summed = jnp.sum(blocks, axis=0)
     return lax.dynamic_slice_in_dim(summed, lax.axis_index("row") * owned_rows, owned_rows, 0)
 
 

time: 414 us -> 592 us (1.43)
  waiting for transfers between devices: 335 us -> 510 us
    all_gather x0 -> x1, waiting for transfers between devices: none -> 345 us  [body(): blocks = lax.all_gather(partial_sum, ('row', 'col'))]
    psum x1 -> x0, waiting for transfers between devices: 170 us -> none  [body(): summed = lax.psum(partial_sum, ('row', 'col'))]
where the time goes in v2:
time: 592 us; the launch traced here: 590 us
  waiting for transfers between devices  510 us (86%)
  local copies, waits for them, and re-layouts  37.6 us (6%)
  other arithmetic  14.8 us (2%)
  between operations  13.4 us (2%)
  starting transfers between devices  11.9 us (2%)
    all_gather x1, waiting for transfers between devices, body(): blocks = lax.all_gather(partial_sum, ('row', 'col'))  345 us
    all_to_all x1, waiting for transfers between devices, body(): lax.all_to_all(cycle_inter, ('row', 'col'), split_axis=0, concat_axis=1,...  165 us
    all_to_all x2, local copies, waits for them, and re-layouts, body(): lax.all_to_all(cycle_inter, ('row', 'col'), split_axis=0, concat_axis=1,...  22.3 us
    unnamed x3, local copies, waits for them, and re-layouts  13.3 us
    all_to_all x1, starting transfers between devices, body(): lax.all_to_all(cycle_inter, ('row', 'col'), split_axis=0, concat_axis=1,...  11.9 us
  transfers between devices with their start and end apart: 2, of which 2 were waited for; matrix products, arithmetic and copies ran while one was open for 0% of the time, Pallas kernels for 0%

profile of v2, /device:TPU:1, one launch (start us, length us, event | category | flops | bytes accessed | tf_op | source)
XLA Modules:
  0.0 590.2 jit_solution(13167373385702013728)
XLA Ops:
  6.5 12.7 %copy.7 = f32[1536,12,128]{2,1,0:T(8,128)} copy(f32[1536,12,128]{2,0,1:T(8,128)} %param.4) | data formatting | bytes 18874368 | tf_op args[0]
  19.2 11.9 %all-to-all-start = ((f32[1536,12,128]{2,1,0:T(8,128)}), f32[1536,12,128]{2,1,0:T(8,128)}, u32[]{:S(2)}, u32[]{:S(2)}) async-start(f32[1536,12,128]{2,1,0:T(8,128)} %copy.7), calls=%async_computation | async-start | bytes 25165824 | tf_op jit(solution)/shard_map/all_to_all | solution.py:13
  31.1 0.0 all-gather.3.cloned.1.call-start
  31.2 165.2 %all-to-all-done = f32[1536,12,128]{2,1,0:T(8,128)} async-done(((f32[1536,12,128]{2,1,0:T(8,128)}), f32[1536,12,128]{2,1,0:T(8,128)}, u32[]{:S(2)}, u32[]{:S(2)}) %all-to-all-start) | async-done | bytes 9437216 | tf_op jit(solution)/shard_map/all_to_all | solution.py:13
  196.3 10.3 %copy.9 = f32[12,128,12,128]{3,2,1,0:T(8,128)} copy(f32[12,128,12,128]{3,2,0,1:T(8,128)} %bitcast.2) | data formatting | bytes 18874368 | tf_op jit(solution)/shard_map/all_to_all | solution.py:13
  206.7 12.0 %all_to_all.16 = f32[12,1536,128]{2,1,0:T(8,128)} reshape(f32[12,128,12,128]{3,2,1,0:T(8,128)} %copy.9) | data formatting | bytes 18874368 | tf_op jit(solution)/shard_map/all_to_all | solution.py:13
  218.7 10.9 %bitcast_subtract_fusion = f32[1536,12,128]{2,0,1:T(8,128)} fusion(f32[1536,12,128]{2,0,1:T(8,128)} %param.4, f32[12,1536,128]{2,1,0:T(8,128)} %all_to_all.16), kind=kLoop, calls=%fused_computation.11 | loop fusion | flops 2359296 | bytes 28311552 | tf_op jit(solution)/shard_map/sub | solution.py:14
  229.6 3.6 while.11
  229.6 1.2 constant_dynamic-slice_fusion.3
  230.8 0.3 copy.15
  231.1 0.1 compare_convert_fusion.2
  231.2 2.1 fusion.12
  233.2 0.0 copy-start
  233.2 0.6 copy-done
  233.9 0.0 all-gather.3.cloned.1.call-update
  233.9 345.1 %all-gather.3.cloned.1.call-done = f32[16384,128]{1,0:T(8,128)} async-done(((f32[128,128]{1,0:T(8,128)}), f32[16384,128]{1,0:T(8,128)}) %all-gather.3.cloned.1.call-update) | async-done | bytes 8388624 | tf_op jit(solution)/shard_map/all_gather | solution.py:36
  579.0 3.8 reduce_sum.9
  582.8 0.6 constant_dynamic-slice_fusion.1
  (3 shorter events, 0.0 us)
Async XLA Ops:
  19.2 177.2 %all-to-all-start = ((f32[1536,12,128]{2,1,0:T(8,128)}), f32[1536,12,128]{2,1,0:T(8,128)}, u32[]{:S(2)}, u32[]{:S(2)}) async-start(f32[1536,12,128]{2,1,0:T(8,128)} %copy.7), calls=%async_computation | async-start | bytes 25165824 | tf_op jit(solution)/shard_map/all_to_all | solution.py:13
  31.1 547.9 %all-gather.3.cloned.1.call-start = ((), (), s32[]{:S(2)}) async-start(), calls=%async_computation.1 | async-start | bytes 8454144 | tf_op jit(solution)/shard_map/all_gather | solution.py:36
  233.2 0.6 copy-start
Sparse Core Ops, SparseCore 0:
  234.0 344.9 all-gather.2
